TPU v7x, 256 devices: a whole 4x4x8 slice. The times are simulated.
256 devices in a mesh: row: 8 (over y, z_hi), col: 32 (over x, z_lo, core).
Axes of the slice: x: 4, y: 4, z: 8 (z_hi: 2, z_lo: 4; z = z_hi * 4 + z_lo), core: 2. Of those that a mesh axis runs over, the one named last changes fastest.
Arguments:
- inputs: bfloat16 [1024, 12288], P('col', 'row'), may hold values from -1.5 to 1.5
- weight: bfloat16 [12288, 49152], P('row', 'col'), may hold values from -0.21875 to 0.21875
- grad_out: bfloat16 [1024, 49152], P('row', 'col'), may hold values from -0.75 to 0.75
Outputs:
- grad_inputs: bfloat16 [1024, 12288], P('col', 'row')
- grad_weight: bfloat16 [12288, 49152], P('row', 'col')
All inputs are finite; a program needn't handle non-finite values.
Results may differ from a plain program's by a relative error of at most 0.0049.
Values may be sent and summed in bfloat16 or wider, within the bound.
A program may use at most 128 MiB of HBM per device.

v0:
```python
import math

import jax
import jax.numpy as jnp
from jax import lax
from jax.sharding import PartitionSpec as P


def gelu_slope(pre):
    coeff = math.sqrt(2.0 / math.pi)
    inner = coeff * (pre + 0.044715 * pre * pre * pre)
    tanh_val = jnp.tanh(inner)
    return 0.5 * (1.0 + tanh_val) + 0.5 * pre * (1.0 - tanh_val * tanh_val) * coeff * (
        1.0 + 3.0 * 0.044715 * pre * pre
    )


def per_device(inputs, weight, grad_out):
    all_inputs = lax.all_gather(inputs, "col", axis=0, tiled=True)
    block = all_inputs
    pre = lax.psum_scatter(
        jnp.dot(block, weight, preferred_element_type=jnp.float32),
        "row",
        scatter_dimension=0,
        tiled=True,
    )
    grad_pre = (grad_out.astype(jnp.float32) * gelu_slope(pre)).astype(jnp.bfloat16)
    all_grad = lax.all_gather(grad_pre, "row", axis=0, tiled=True)
    grad_weight = lax.dot_general(
        all_inputs, all_grad, (((0,), (0,)), ((), ())), preferred_element_type=jnp.float32
    ).astype(jnp.bfloat16)
    block = all_grad
    grad_inputs = lax.psum_scatter(
        lax.dot_general(
            block, weight, (((1,), (1,)), ((), ())), preferred_element_type=jnp.float32
        ),
        "col",
        scatter_dimension=0,
        tiled=True,
    ).astype(jnp.bfloat16)
    return (grad_inputs, grad_weight)


def solution(mesh):
    return jax.shard_map(
        per_device,
        mesh=mesh,
        in_specs=(P("col", "row"), P("row", "col"), P("row", "col")),
        out_specs=(P("col", "row"), P("row", "col")),
        check_vma=False,
    )
```

profile of v0, /device:TPU:1, one launch (start us, length us, event | category | flops | bytes accessed | tf_op | source)
XLA Modules:
  0.0 496.1 jit_solution(7478155835027388425)
XLA Ops:
  7.2 0.0 all-gather.3.cloned.1.call-start
  7.2 0.7 all-gather.3.cloned.1.call-update
  7.9 0.0 reduce-scatter.3.cloned.1.call-start
  7.9 67.7 %all-gather.3.cloned.1.call-done = bf16[1024,1536]{1,0:T(8,128)(2,1)} async-done(((bf16[32,1536]{1,0:T(8,128)(2,1)}), bf16[1024,1536]{1,0:T(8,128)(2,1)}) %all-gather.3.cloned.1.call-update) | async-done | bytes 3145744 | tf_op jit(solution)/shard_map/all_gather | solution.py:19
  75.6 9.7 %fusion.8 = f32[1024,1536]{1,0:T(8,128)} fusion(bf16[1024,1536]{1,0:T(8,128)(2,1)} %all-gather.3.cloned.1.call-done, bf16[1536,1536]{1,0:T(8,128)(2,1)} %param.4), kind=kOutput, calls=%fused_computation.11 | convolution fusion | flops 4831838208 | bytes 14155776 | tf_op jit(solution)/shard_map/dot_general | solution.py:22
  85.3 0.0 copy-start
  85.3 0.0 reduce-scatter.3.cloned.1.call-update
  85.4 0.0 all-gather.5.cloned.1.call-start
  85.4 151.1 %reduce-scatter.3.cloned.1.call-done = f32[128,1536]{1,0:T(8,128)} async-done(((f32[1024,1536]{1,0:T(8,128)}), f32[128,1536]{1,0:T(8,128)}) %reduce-scatter.3.cloned.1.call-update) | async-done | bytes 786448 | tf_op jit(solution)/shard_map/reduce_scatter | solution.py:21
  236.5 0.0 copy-done
  236.5 2.4 fusion.7
  238.9 0.0 all-gather.5.cloned.1.call-update
  239.0 0.0 reduce-scatter.5.cloned.1.call-start
  239.0 89.8 %all-gather.5.cloned.1.call-done = bf16[1024,1536]{1,0:T(8,128)(2,1)} async-done(((bf16[128,1536]{1,0:T(8,128)(2,1)}), bf16[1024,1536]{1,0:T(8,128)(2,1)}) %all-gather.5.cloned.1.call-update) | async-done | bytes 3145744 | tf_op jit(solution)/shard_map/all_gather | solution.py:28
  328.9 9.8 %fusion.9 = f32[1024,1536]{1,0:T(8,128)} fusion(bf16[1024,1536]{1,0:T(8,128)(2,1)} %all-gather.5.cloned.1.call-done, bf16[1536,1536]{1,0:T(8,128)(2,1)} %param.4), kind=kOutput, calls=%fused_computation.12 | convolution fusion | flops 4831838208 | bytes 14155776 | tf_op jit(solution)/shard_map/dot_general | solution.py:34
  338.6 0.0 copy-start.1
  338.6 0.0 reduce-scatter.5.cloned.1.call-update
  338.7 1.9 copy-done.1
  340.5 8.8 %fusion = bf16[1536,1536]{0,1:T(8,128)(2,1)} fusion(bf16[1024,1536]{1,0:T(8,128)(2,1)} %all-gather.5.cloned.1.call-done, bf16[1024,1536]{1,0:T(8,128)(2,1)S(1)} %copy-done.1), kind=kOutput, calls=%fused_computation.1 | convolution fusion | flops 4834197504 | bytes 11010048 | tf_op jit(solution)/shard_map/dot_general | solution.py:29
  349.3 6.6 %copy.5 = bf16[1536,1536]{1,0:T(8,128)(2,1)} copy(bf16[1536,1536]{0,1:T(8,128)(2,1)} %fusion) | data formatting | bytes 9437184
  356.0 132.0 %reduce-scatter.5.cloned.1.call-done = f32[32,1536]{1,0:T(8,128)} async-done(((f32[1024,1536]{1,0:T(8,128)}), f32[32,1536]{1,0:T(8,128)}) %reduce-scatter.5.cloned.1.call-update) | async-done | bytes 196624 | tf_op jit(solution)/shard_map/reduce_scatter | solution.py:33
  487.9 1.6 convert_element_type.17
Async XLA Ops:
  7.2 68.4 %all-gather.3.cloned.1.call-start = ((), (), s32[]{:S(2)}) async-start(), calls=%async_computation.2 | async-start | bytes 3244032 | tf_op jit(solution)/shard_map/all_gather | solution.py:19
  7.9 228.6 %reduce-scatter.3.cloned.1.call-start = ((), (), s32[]{:S(2)}) async-start(), calls=%async_computation.3 | async-start | bytes 7077888 | tf_op jit(solution)/shard_map/reduce_scatter | solution.py:21
  85.3 151.2 %copy-start = (bf16[128,1536]{1,0:T(8,128)(2,1)S(1)}, bf16[128,1536]{1,0:T(8,128)(2,1)}, u32[]{:S(2)}) copy-start(bf16[128,1536]{1,0:T(8,128)(2,1)} %param.5) | copy-start | bytes 1179652
  85.4 243.5 %all-gather.5.cloned.1.call-start = ((), (), s32[]{:S(2)}) async-start(), calls=%async_computation.4 | async-start | bytes 3538944 | tf_op jit(solution)/shard_map/all_gather | solution.py:28
  239.0 249.0 %reduce-scatter.5.cloned.1.call-start = ((), (), s32[]{:S(2)}) async-start(), calls=%async_computation.5 | async-start | bytes 6488064 | tf_op jit(solution)/shard_map/reduce_scatter | solution.py:33
  338.6 1.9 copy-start.1
Sparse Core Ops, SparseCore 0:
  9.9 65.7 all-gather.2
  85.5 151.0 reduce-scatter.2
  240.1 88.7 all-gather.4
  338.8 149.1 reduce-scatter.4
where the time goes:
time: 499 us; the launch traced here: 496 us
  waiting for transfers between devices  441 us (88%)
  matrix products  28.3 us (6%)
  between operations  13.8 us (3%)
  local copies, waits for them, and re-layouts  8.5 us (2%)
    reduce_scatter x1, waiting for transfers between devices, per_device(): lax.psum_scatter(jnp.dot(block, weight, preferred_element_type=jnp.float3...  151 us
    reduce_scatter x1, waiting for transfers between devices, per_device(): lax.psum_scatter(lax.dot_general(block, weight, (((1,), (1,)), ((), ())),...  132 us
    all_gather x1, waiting for transfers between devices, per_device(): all_grad = lax.all_gather(grad_pre, 'row', axis=0, tiled=True)  89.8 us
    all_gather x1, waiting for transfers between devices, per_device(): all_inputs = lax.all_gather(inputs, 'col', axis=0, tiled=True)  67.7 us
  transfers between devices with their start and end apart: 4, of which 4 were waited for; matrix products, arithmetic and copies ran while one was open for 3% of the time, Pallas kernels for 0%

commit v1 on v0

v1 whole, which is shorter than its diff:
```python
import math

import jax
import jax.numpy as jnp
from jax import lax
from jax.experimental import pallas as pl
from jax.experimental.pallas import tpu as pltpu
from jax.sharding import PartitionSpec as P

MESH = pl.DeviceIdType.MESH
NB = 4
BLK = 16
BF = jnp.bfloat16
F32 = jnp.float32
TILE = 256

OFF = dict(z=0, a=1, c=2, d=3, e=4, f=5, g=6, h=7, i=8, j=9, k=10, l=11, m=12)
NSLOTS = OFF["m"] + NB
GW_FIRST = OFF["j"] + NB - 1


def gelu_slope(pre):
    coeff = math.sqrt(2.0 / math.pi)
    inner = coeff * (pre + 0.044715 * pre * pre * pre)
    tanh_val = jnp.tanh(inner)
    return 0.5 * (1.0 + tanh_val) + 0.5 * pre * (1.0 - tanh_val * tanh_val) * coeff * (
        1.0 + 3.0 * 0.044715 * pre * pre
    )


def kernel(
    inp, w_hbm, go_hbm,
    out, gw_hbm,
    w, go, xs, p32, pb, a_in, bc_in, s_keep, zs, z_in, gp, g32, sib_out, sib_in,
    x_out, x_in, x_keep, t_out, t_in, gwb,
    lsem, wsem, gsem, gwsem,
    zi_s, zi_r, xi_s, xi_r, si_s, si_r, a_s, a_r, b_s, b_r, c_s, c_r, zr_s, zr_r, zg_s, zg_r,
    ga_s, ga_r, gb_s, gb_r, gc_s, gc_r, so_s, so_r, xo_s, xo_r, zo_s, zo_r,
):
    row = lax.axis_index("row")
    col = lax.axis_index("col")
    y, zh = row // 2, row % 2
    x, zl, k = col // 8, (col // 2) % 4, col % 2

    def dev(y=y, zh=zh, x=x, zl=zl, k=k):
        return (y * 2 + zh, (x * 4 + zl) * 2 + k)

    yp, ym = (y + 1) % 4, (y + 3) % 4
    yo = (y + 2) % 4
    d_yp, d_ym = dev(y=yp), dev(y=ym)
    d_zh = dev(zh=1 - zh)
    d_sib = dev(k=1 - k)

    def d_x(d):
        return dev(x=(x + d) % 4)

    def d_z(d):
        return dev(zl=(zl + d) % 4)

    def rc(src, dst, ss, rs, to):
        return pltpu.make_async_remote_copy(
            src_ref=src, dst_ref=dst, send_sem=ss, recv_sem=rs, device_id=to, device_id_type=MESH
        )

    w_cp = pltpu.make_async_copy(w_hbm, w, wsem)
    go_cp = pltpu.make_async_copy(go_hbm, go, gsem)
    w_cp.start()
    go_cp.start()

    barrier = pltpu.get_barrier_semaphore()
    partners = [d_yp, d_ym, d_zh, d_sib] + [d_x(d) for d in (1, 2, 3)] + [d_z(d) for d in (1, 2, 3)]
    for to in partners:
        pl.semaphore_signal(barrier, inc=1, device_id=to, device_id_type=MESH)
    pl.semaphore_wait(barrier, len(partners))

    def gk(g, kk):
        return pl.ds((g * 2 + kk) * 2, 2)

    def zi(b, d):
        return rc(inp.at[b // 2], xs.at[b, (x * 2 + k) * 2 + zl // 2], zi_s.at[b, d - 1], zi_r.at[b, zl // 2], d_z(d))

    def zi_wait(b, h):
        r = xs.at[b, (x * 2 + k) * 2 + h]
        return rc(r, r, zi_s.at[b, 0], zi_r.at[b, h], d_z(1))

    def own_copy(b):
        return pltpu.make_async_copy(inp.at[b // 2], xs.at[b, (x * 2 + k) * 2 + zl // 2], lsem.at[b])

    def xi(b, d):
        r = xs.at[b, gk(x, k)]
        return rc(r, r, xi_s.at[b, d - 1], xi_r.at[b, d - 1], d_x(d))

    def si(b, d):
        r = xs.at[b, gk((x + d) % 4, k)]
        return rc(r, r, si_s.at[b, d], si_r.at[b, d], d_sib)

    def a_cp(b, n):
        return rc(pb.at[b, gk(yo, n)], a_in.at[b, n], a_s.at[b, n], a_r.at[b, n], (d_yp, d_ym)[n])

    def b_cp(b, n):
        return rc(
            pb.at[b, gk((yp, ym)[n], 1 - n)], bc_in.at[b, n, 1 - n], b_s.at[b, n], b_r.at[b, n], (d_yp, d_ym)[n]
        )

    def c_cp(b, n):
        return rc(pb.at[b, gk((yp, ym)[n], n)], bc_in.at[b, n, n], c_s.at[b, n], c_r.at[b, n], (d_yp, d_ym)[n])

    def zr(b):
        return rc(zs.at[b], z_in.at[b], zr_s.at[b], zr_r.at[b], d_zh)

    def zg(b, kk):
        r = gp.at[b, (y * 2 + kk) * 2 + zh]
        return rc(r, r, zg_s.at[b, kk], zg_r.at[b, kk], d_zh)

    def ga(b, n):
        r = gp.at[b, gk(y, n)]
        return rc(r, r, ga_s.at[b, n], ga_r.at[b, n], (d_yp, d_ym)[n])

    def gb(b, n):
        r = gp.at[b, gk(y, 1 - n)]
        return rc(r, r, gb_s.at[b, n], gb_r.at[b, n], (d_yp, d_ym)[n])

    def gc(b, n):
        r = gp.at[b, gk((ym, yp)[n], n)]
        return rc(r, r, gc_s.at[b, n], gc_r.at[b, n], (d_yp, d_ym)[n])

    def so(b):
        return rc(sib_out.at[b], sib_in.at[b], so_s.at[b], so_r.at[b], d_sib)

    def xo(b, d):
        return rc(x_out.at[b, d - 1], x_in.at[b, d - 1], xo_s.at[b, d - 1], xo_r.at[b, d - 1], d_x(d))

    def zo(b, d):
        return rc(t_out.at[b, d - 1], t_in.at[b, d - 1], zo_s.at[b, d - 1], zo_r.at[b, d - 1], d_z(d))

    def st_z(b):
        @pl.when(zl % 2 == b % 2)
        def _():
            for d in (1, 2, 3):
                zi(b, d).start()
            own_copy(b).start()

    def st_a(b):
        for h in range(2):
            @pl.when(zl != 2 * h + b % 2)
            def _():
                zi_wait(b, h).wait_recv()

            @pl.when(zl == 2 * h + b % 2)
            def _():
                own_copy(b).wait()
        for d in (1, 3, 2):
            xi(b, d).start()
        si(b, 0).start()

    def st_c(b):
        for d in (1, 3, 2):
            xi(b, d).wait_recv()
            si(b, 4 - d).start()

    def st_d(b):
        for d in range(4):
            si(b, d).wait_recv()

        @pl.when(b == 0)
        def _():
            w_cp.wait()

        @pl.loop(0, 1536 // TILE)
        def _(t):
            cols = pl.ds(pl.multiple_of(t * TILE, TILE), TILE)
            acc = jnp.dot(xs[b].reshape(256, 1536), w[:, cols], preferred_element_type=F32).reshape(16, BLK, TILE)
            p32[b, :, :, cols] = acc
            pb[b, :, :, cols] = acc.astype(BF)

        for n in range(2):
            a_cp(b, n).start()
        for n in range(2):
            b_cp(b, n).start()

    def st_e(b):
        for n in range(2):
            a_cp(b, n).wait_recv()
            r = gk((yp, ym)[n], n)
            pb[b, r] = (p32[b, r] + a_in[b, n].astype(F32)).astype(BF)
            c_cp(b, n).start()

    def st_f(b):
        for n in range(2):
            b_cp(b, n).wait_recv()
        for n in range(2):
            c_cp(b, n).wait_recv()
        for kk in range(2):
            def total(h):
                return (
                    p32[b, (y * 2 + kk) * 2 + h]
                    + bc_in[b, 0, kk, h].astype(F32)
                    + bc_in[b, 1, kk, h].astype(F32)
                )
            s_keep[b, kk] = total(zh)
            zs[b, kk] = total(1 - zh).astype(BF)
        zr(b).start()

    def st_g(b):
        @pl.when(b == 0)
        def _():
            go_cp.wait()

        zr(b).wait_recv()
        for kk in range(2):
            pre = s_keep[b, kk] + z_in[b, kk].astype(F32)
            gp[b, (y * 2 + kk) * 2 + zh] = (go[b % 2, kk, b // 2].astype(F32) * gelu_slope(pre)).astype(BF)
            zg(b, kk).start()

    def st_h(b):
        for kk in range(2):
            r = gp.at[b, (y * 2 + kk) * 2 + 1 - zh]
            rc(r, r, zg_s.at[b, kk], zg_r.at[b, kk], d_zh).wait_recv()
        for n in range(2):
            ga(b, n).start()
        for n in range(2):
            gb(b, n).start()

    def st_i(b):
        for n in range(2):
            r = gp.at[b, gk((ym, yp)[n], n)]
            rc(r, r, ga_s.at[b, n], ga_r.at[b, n], (d_yp, d_ym)[n]).wait_recv()
            gc(b, n).start()

    def st_j(b):
        for n in range(2):
            r = gp.at[b, gk((ym, yp)[n], 1 - n)]
            rc(r, r, gb_s.at[b, n], gb_r.at[b, n], (d_yp, d_ym)[n]).wait_recv()
        for n in range(2):
            r = gp.at[b, gk(yo, n)]
            rc(r, r, gc_s.at[b, n], gc_r.at[b, n], (d_yp, d_ym)[n]).wait_recv()

        @pl.loop(0, 1536 // TILE)
        def _(t):
            o = pl.multiple_of(t * TILE, TILE)
            acc = lax.dot_general(
                gp[b].reshape(256, 1536), w[pl.ds(o, TILE), :], (((1,), (1,)), ((), ())), preferred_element_type=F32
            )
            g32[b, :, :, pl.ds(o, TILE)] = acc.reshape(16, BLK, TILE)

        for g in range(4):
            sib_out[b, pl.ds(2 * g, 2)] = g32[b, gk(g, 1 - k)].astype(BF)
        so(b).start()

    def st_k(b):
        so(b).wait_recv()

        def total(g):
            return g32[b, gk(g, k)] + sib_in[b, pl.ds(2 * g, 2)].astype(F32)

        for d in (1, 3, 2):
            x_out[b, d - 1] = total((x + d) % 4).astype(BF)
            xo(b, d).start()
        x_keep[b] = total(x)

    def st_l(b):
        for d in (1, 3, 2):
            xo(b, d).wait_recv()
        for h in range(2):
            tot = x_keep[b, h]
            for d in range(3):
                tot = tot + x_in[b, d, h].astype(F32)
            x_keep[b, h] = tot
            to = 2 * h + b % 2
            for d in (1, 2, 3):
                @pl.when((zl + d) % 4 == to)
                def _():
                    t_out[b, d - 1] = x_keep[b, h].astype(BF)
                    zo(b, d).start()

    def st_m(b):
        @pl.when(zl % 2 == b % 2)
        def _():
            tot = x_keep[b, zl // 2]
            for d in (1, 2, 3):
                zo(b, d).wait_recv()
            for d in range(3):
                tot = tot + t_in[b, d].astype(F32)
            out[b // 2] = tot.astype(BF)

    def gw_out(t):
        rows = pl.ds(t * TILE if isinstance(t, int) else pl.multiple_of(t * TILE, TILE), TILE)
        return pltpu.make_async_copy(gwb.at[rows], gw_hbm.at[rows], gwsem.at[t])

    def gw_tile(t):
        o = pl.multiple_of(t * TILE, TILE)
        acc = lax.dot_general(
            xs[:, :, :, pl.ds(o, TILE)].reshape(1024, TILE),
            gp[...].reshape(1024, 1536),
            (((0,), (0,)), ((), ())),
            preferred_element_type=F32,
        )
        gwb[pl.ds(o, TILE), :] = acc.astype(BF)
        gw_out(t).start()

    stages = dict(z=st_z, a=st_a, c=st_c, d=st_d, e=st_e, f=st_f, g=st_g, h=st_h, i=st_i, j=st_j, k=st_k, l=st_l, m=st_m)

    @pl.loop(0, NSLOTS)
    def _(slot):
        for name in "mlkjihgfedcaz":
            b = slot - OFF[name]

            @pl.when((b >= 0) & (b < NB))
            def _():
                stages[name](b)

        @pl.when((slot >= GW_FIRST) & (slot < GW_FIRST + 3))
        def _():
            @pl.loop(0, 2)
            def _(t):
                gw_tile((slot - GW_FIRST) * 2 + t)

    @pl.loop(0, NB)
    def _(b):
        @pl.when(zl % 2 == b % 2)
        def _():
            for d in (1, 2, 3):
                zi(b, d).wait_send()
        for d in (1, 2, 3):
            xi(b, d).wait_send()
            xo(b, d).wait_send()

            @pl.when((zl + d) % 2 == b % 2)
            def _():
                zo(b, d).wait_send()
        for d in range(4):
            si(b, d).wait_send()
        for n in range(2):
            for cp in (a_cp, b_cp, c_cp, zg, ga, gb, gc):
                cp(b, n).wait_send()
        zr(b).wait_send()
        so(b).wait_send()

    for t in range(6):
        gw_out(t).wait()


def per_device(inputs, weight, grad_out):
    any_ = pl.BlockSpec(memory_space=pl.ANY)
    vmem = pl.BlockSpec(memory_space=pltpu.VMEM)
    V = pltpu.VMEM
    D = pltpu.SemaphoreType.DMA
    sems = []
    for shape in (
        (NB, 3), (NB, 2),
        (NB, 3), (NB, 3),
        (NB, 4), (NB, 4),
        (NB, 2), (NB, 2), (NB, 2), (NB, 2), (NB, 2), (NB, 2),
        (NB,), (NB,),
        (NB, 2), (NB, 2),
        (NB, 2), (NB, 2), (NB, 2), (NB, 2), (NB, 2), (NB, 2),
        (NB,), (NB,),
        (NB, 3), (NB, 3),
        (NB, 3), (NB, 3),
    ):
        sems.append(D(shape))
    grad_inputs, grad_weight = pl.pallas_call(
        kernel,
        out_shape=(
            jax.ShapeDtypeStruct((2, BLK, 1536), BF),
            jax.ShapeDtypeStruct((1536, 1536), BF),
        ),
        in_specs=[vmem, any_, any_],
        out_specs=(vmem, any_),
        scratch_shapes=[
            V((1536, 1536), BF),
            V((2, 2, 2, BLK, 1536), BF),
            V((NB, 16, BLK, 1536), BF),
            V((NB, 16, BLK, 1536), F32),
            V((NB, 16, BLK, 1536), BF),
            V((NB, 2, 2, BLK, 1536), BF),
            V((NB, 2, 2, 2, BLK, 1536), BF),
            V((NB, 2, BLK, 1536), F32),
            V((NB, 2, BLK, 1536), BF),
            V((NB, 2, BLK, 1536), BF),
            V((NB, 16, BLK, 1536), BF),
            V((NB, 16, BLK, 1536), F32),
            V((NB, 8, BLK, 1536), BF),
            V((NB, 8, BLK, 1536), BF),
            V((NB, 3, 2, BLK, 1536), BF),
            V((NB, 3, 2, BLK, 1536), BF),
            V((NB, 2, BLK, 1536), F32),
            V((NB, 3, BLK, 1536), BF),
            V((NB, 3, BLK, 1536), BF),
            V((1536, 1536), BF),
            D((NB,)), D, D, D((6,)),
            *sems,
        ],
        compiler_params=pltpu.CompilerParams(
            collective_id=0, has_side_effects=True, vmem_limit_bytes=60 * 2**20
        ),
        cost_estimate=pl.CostEstimate(flops=3 * 2 * 1024 * 1536 * 1536, bytes_accessed=10**7, transcendentals=128 * 1536),
    )(inputs.reshape(2, BLK, 1536), weight, grad_out.reshape(2, 2, 2, BLK, 1536))
    return grad_inputs.reshape(32, 1536), grad_weight


def solution(mesh):
    return jax.shard_map(
        per_device,
        mesh=mesh,
        in_specs=(P("col", "row"), P("row", "col"), P("row", "col")),
        out_specs=(P("col", "row"), P("row", "col")),
        check_vma=False,
    )
```

time: 499 us -> 114 us (0.23)
  waiting for transfers between devices: 441 us -> 0 us
  Pallas kernels: 0 us -> 107 us
  matrix products: 28.3 us -> 0 us
  between operations: 13.8 us -> 0.64 us
    reduce_scatter x2 -> x0, waiting for transfers between devices: 283 us -> none  [the longest x1 151 us: per_device(): lax.psum_scatter(jnp.dot(block, weight, preferred_element_type=jnp.float3...]
    all_gather x2 -> x0, waiting for transfers between devices: 158 us -> none  [the longest x1 89.8 us: per_device(): all_grad = lax.all_gather(grad_pre, 'row', axis=0, tiled=True)]
    pallas_call x0 -> x1, Pallas kernels: none -> 107 us  [per_device(): pl.pallas_call(kernel, out_shape=(jax.ShapeDtypeStruct((2, BLK, 1536), BF...]
    dot_general x3 -> x0, matrix products: 28.3 us -> none  [the longest x1 9.78 us: per_device(): lax.dot_general(block, weight, (((1,), (1,)), ((), ())), preferred_elemen...]
  transfers between devices with their start and end apart: 4 -> 0, of which waited for: 4 -> 0; matrix products, arithmetic and copies ran while one was open for 3% -> 0% of each run, Pallas kernels for 0% -> 0%
where the time goes in v1:
time: 114 us
  Pallas kernels  107 us (94%)
  local copies, waits for them, and re-layouts  6.36 us (6%)
    pallas_call x1, Pallas kernels, per_device(): pl.pallas_call(kernel, out_shape=(jax.ShapeDtypeStruct((2, BLK, 1536), BF...  107 us
    unnamed x2, local copies, waits for them, and re-layouts  6.36 us

profile of v1, /device:TPU:1, one launch (start us, length us, event | category | flops | bytes accessed | tf_op | source)
XLA Modules:
  0.0 113.6 jit_solution(17332583565440084072)
XLA Ops:
  0.6 106.6 %shard_map.50 = (bf16[2,16,1536]{2,1,0:T(8,128)(2,1)}, bf16[1536,1536]{1,0:T(8,128)(2,1)}) custom-call(bf16[2,16,1536]{2,1,0:T(8,128)(2,1)} %bitcast.5, bf16[1536,1536]{1,0:T(8,128)(2,1)} %w_hbm.1, bf16[2,2,2,16,1536]{4,3,2,1,0:T(8,128)(2,1)} %bitcast.4), custom_call_target="tpu_custom_call" | custom-call | flops 14495514624 | bytes 10000000 | tf_op jit(solution)/shard_map/pallas_call | solution.py:362
  107.2 1.5 %copy.7 = bf16[32,1536]{1,0:T(8,128)(2,1)} copy(bf16[32,1536]{1,0:T(8,128)(2,1)} %bitcast.3) | data formatting | bytes 196608
  108.8 4.8 %copy.8 = bf16[1536,1536]{1,0:T(8,128)(2,1)} copy(bf16[1536,1536]{1,0:T(8,128)(2,1)} %get-tuple-element.9) | data formatting | bytes 9437184

commit v2 on v0

v2 whole, which is shorter than its diff:
```python
import math

import jax
import jax.numpy as jnp
from jax import lax
from jax.experimental import pallas as pl
from jax.experimental.pallas import tpu as pltpu
from jax.sharding import PartitionSpec as P

MESH = pl.DeviceIdType.MESH
NB = 4
BLK = 16
BF = jnp.bfloat16
F32 = jnp.float32
TILE = 256

PIECES = 8
HALF = 768
NS = 2 * NB

ORDER = (('h', 13), ('e', 8), ('l', 21), ('j', 17), ('g', 11), ('k', 18), ('m', 37), ('i', 14), ('f', 9), ('d', 6), ('a', 2), ('c', 5), ('z', 0))
DRY = {'d': 5, 'j': 6}
NSLOTS = max(first for _, first in ORDER) + NS
GW_FIRST = dict(ORDER)["j"] + NS - 1
GW_EACH = 2


def gelu_slope(pre):
    coeff = math.sqrt(2.0 / math.pi)
    inner = coeff * (pre + 0.044715 * pre * pre * pre)
    tanh_val = jnp.tanh(inner)
    return 0.5 * (1.0 + tanh_val) + 0.5 * pre * (1.0 - tanh_val * tanh_val) * coeff * (
        1.0 + 3.0 * 0.044715 * pre * pre
    )


def kernel(
    inp, w_hbm, go_hbm,
    out, gw_hbm,
    w, go, xs, p32, pb, a_in, bc_in, s_keep, zs, z_in, gp, g32, sib_out, sib_in,
    x_out, x_in, x_keep, t_out, t_in, gwb,
    lsem, wsem, gsem, gwsem,
    zi_s, zi_r, xi_s, xi_r, si_s, si_r, abc_s, a_r, bc_r, zr_s, zr_r, zg_s, zg_r, g_s, ga_r, gbc_r,
    so_s, so_r, xo_s, xo_r, zo_s, zo_r,
):
    row = lax.axis_index("row")
    col = lax.axis_index("col")
    y, zh = row // 2, row % 2
    x, zl, k = col // 8, (col // 2) % 4, col % 2

    def dev(y=y, zh=zh, x=x, zl=zl, k=k):
        return (y * 2 + zh, (x * 4 + zl) * 2 + k)

    yp, ym = (y + 1) % 4, (y + 3) % 4
    yo = (y + 2) % 4
    d_yp, d_ym = dev(y=yp), dev(y=ym)
    d_zh = dev(zh=1 - zh)
    d_sib = dev(k=1 - k)

    def d_x(d):
        return dev(x=(x + d) % 4)

    def d_z(d):
        return dev(zl=(zl + d) % 4)

    def rc(src, dst, ss, rs, to):
        return pltpu.make_async_remote_copy(
            src_ref=src, dst_ref=dst, send_sem=ss, recv_sem=rs, device_id=to, device_id_type=MESH
        )

    w_cp = pltpu.make_async_copy(w_hbm, w, wsem)
    go_cp = pltpu.make_async_copy(go_hbm, go, gsem)
    w_cp.start()
    go_cp.start()

    barrier = pltpu.get_barrier_semaphore()
    partners = [d_yp, d_ym, d_zh, d_sib] + [d_x(d) for d in (1, 2, 3)] + [d_z(d) for d in (1, 2, 3)]
    for to in partners:
        pl.semaphore_signal(barrier, inc=1, device_id=to, device_id_type=MESH)
    pl.semaphore_wait(barrier, len(partners))

    def gk(g, kk):
        return pl.ds((g * 2 + kk) * 2, 2)

    def sent(region, sem):
        rc(region, region, sem, so_r.at[0], d_sib).wait_send()

    def arrived(region, sem):
        rc(region, region, so_s, sem, d_sib).wait_recv()

    def part(b):
        return ((b + 1) // 2) % 2

    def source(b, h):
        return (2 + part(b)) if h else (1 - part(b))

    def mine(b):
        return ((zl + 1) // 2) % 2 != part(b)

    def zi(b, d):
        return rc(inp.at[b // 2], xs.at[b, x, k, zl // 2], zi_s.at[b], zi_r.at[b, zl // 2], d_z(d))

    def own_copy(b):
        return pltpu.make_async_copy(inp.at[b // 2], xs.at[b, x, k, zl // 2], lsem.at[b])

    def xi(b, d):
        r = xs.at[b, x, k]
        return rc(r, r, xi_s, xi_r.at[b], d_x(d))

    def si(b):
        r = xs.at[b, :, k]
        return rc(r, r, si_s, si_r.at[b], d_sib)

    def a_cp(n, i):
        return rc(pb.at[n, gk(yo, i)], a_in.at[n, i], abc_s, a_r.at[n, i], (d_yp, d_ym)[i])

    def b_cp(n, i):
        return rc(pb.at[n, gk((yp, ym)[i], 1 - i)], bc_in.at[n, i, 1 - i], abc_s, bc_r.at[n], (d_yp, d_ym)[i])

    def c_cp(n, i):
        return rc(pb.at[n, gk((yp, ym)[i], i)], bc_in.at[n, i, i], abc_s, bc_r.at[n], (d_yp, d_ym)[i])

    def zr(n):
        return rc(zs.at[n], z_in.at[n], zr_s, zr_r.at[n], d_zh)

    def zg(n):
        r = gp.at[n, y, :, zh]
        return rc(r, r, zg_s, zg_r.at[n], d_zh)

    def ga(n, i):
        r = gp.at[n, y, i]
        return rc(r, r, g_s, ga_r.at[n, i], (d_yp, d_ym)[i])

    def gb(n, i):
        r = gp.at[n, y, 1 - i]
        return rc(r, r, g_s, gbc_r.at[n // 2], (d_yp, d_ym)[i])

    def gc(n, i):
        r = gp.at[n, (ym, yp)[i], i]
        return rc(r, r, g_s, gbc_r.at[n // 2], (d_yp, d_ym)[i])

    def so(n):
        return rc(sib_out.at[n], sib_in.at[n], so_s, so_r.at[n], d_sib)

    def xo(n, d):
        return rc(x_out.at[n, d - 1], x_in.at[n, d - 1], xo_s, xo_r.at[n], d_x(d))

    def zo(n, d):
        return rc(t_out.at[n, d - 1], t_in.at[n, d - 1], zo_s.at[n], zo_r.at[n], d_z(d))

    def half(q, t=0, size=HALF):
        return pl.ds(pl.multiple_of(q * HALF + t * size, size), size)

    def st_z(b):
        @pl.when(mine(b))
        def _():
            for d in (1, 2, 3):
                zi(b, d).start()
            own_copy(b).start()

    def st_a(b):
        for h in range(2):
            @pl.when(zl != source(b, h))
            def _():
                arrived(xs.at[b, x, k, h], zi_r.at[b, h])

            @pl.when(zl == source(b, h))
            def _():
                own_copy(b).wait()
        for d in (1, 3, 2):
            xi(b, d).start()

    def st_c(b):
        arrived(xs.at[b, pl.ds(0, 3), k], xi_r.at[b])
        si(b).start()

    def st_d(n):
        b, q = n // 2, n % 2

        @pl.when((q == 0) & (n < NS))
        def _():
            arrived(xs.at[b, :, 1 - k], si_r.at[b])

        @pl.when(n == NS)
        def _():
            w_cp.wait()

        @pl.loop(0, jnp.where(n < NS, HALF // TILE, 1))
        def _(t):
            cols = pl.ds(pl.multiple_of(t * TILE, TILE), TILE)
            acc = jnp.dot(xs[b].reshape(256, 1536), w[:, half(q, t, TILE)], preferred_element_type=F32)
            acc = acc.reshape(16, BLK, TILE)
            p32[n, :, :, cols] = acc
            pb[n, :, :, cols] = acc.astype(BF)

        @pl.when(n < NS)
        def _():
            for i in range(2):
                a_cp(n, i).start()
            for i in range(2):
                b_cp(n, i).start()

    def st_e(n):
        for i in range(2):
            arrived(a_in.at[n, i], a_r.at[n, i])
            r = gk((yp, ym)[i], i)
            pb[n, r] = (p32[n, r] + a_in[n, i].astype(F32)).astype(BF)
            c_cp(n, i).start()

    def st_f(n):
        arrived(bc_in.at[n], bc_r.at[n])
        for kk in range(2):
            def total(h):
                return (
                    p32[n, (y * 2 + kk) * 2 + h]
                    + bc_in[n, 0, kk, h].astype(F32)
                    + bc_in[n, 1, kk, h].astype(F32)
                )
            s_keep[n, kk] = total(zh)
            zs[n, kk] = total(1 - zh).astype(BF)
        zr(n).start()

    def st_g(n):
        b, q = n // 2, n % 2

        @pl.when(n == 0)
        def _():
            go_cp.wait()

        arrived(z_in.at[n], zr_r.at[n])
        line = part(b) * zh + (1 - part(b)) * (1 - zh)
        for kk in range(2):
            pre = s_keep[n, kk] + z_in[n, kk].astype(F32)
            cot = go[line, kk, b // 2, :, half(q)].astype(F32)
            gp[n, y, kk, zh] = (cot * gelu_slope(pre)).astype(BF)
        zg(n).start()

    def st_h(n):
        arrived(gp.at[n, y, :, 1 - zh], zg_r.at[n])
        for i in range(2):
            ga(n, i).start()
        for i in range(2):
            gb(n, i).start()

    def st_i(n):
        for i in range(2):
            arrived(gp.at[n, (ym, yp)[i], i], ga_r.at[n, i])
            gc(n, i).start()

    def st_j(n):
        b, q = n // 2, n % 2

        @pl.when((q == 0) & (n < NS))
        def _():
            arrived(gp.at[pl.ds(2 * b, 2), pl.ds(0, 2)], gbc_r.at[b])

        @pl.loop(0, jnp.where(n < NS, HALF // TILE, 1))
        def _(t):
            rows = half(q, t, TILE)
            acc = 0.0
            for p in range(2):
                acc += lax.dot_general(
                    gp[2 * b + p].reshape(256, HALF),
                    w[rows, p * HALF : (p + 1) * HALF],
                    (((1,), (1,)), ((), ())),
                    preferred_element_type=F32,
                )
            g32[n, :, :, pl.ds(pl.multiple_of(t * TILE, TILE), TILE)] = acc.reshape(16, BLK, TILE)

        @pl.when(n < NS)
        def _():
            for g in range(4):
                sib_out[n, pl.ds(2 * g, 2)] = g32[n, gk(g, 1 - k)].astype(BF)
            so(n).start()

    def st_k(n):
        arrived(sib_in.at[n], so_r.at[n])

        def total(g):
            return g32[n, gk(g, k)] + sib_in[n, pl.ds(2 * g, 2)].astype(F32)

        for d in (1, 3, 2):
            x_out[n, d - 1] = total((x + d) % 4).astype(BF)
            xo(n, d).start()
        x_keep[n] = total(x)

    def st_l(n):
        b = n // 2
        arrived(x_in.at[n], xo_r.at[n])
        for h in range(2):
            tot = x_keep[n, h]
            for d in range(3):
                tot = tot + x_in[n, d, h].astype(F32)
            x_keep[n, h] = tot
            to = source(b, h)
            for d in (1, 2, 3):
                @pl.when((zl + d) % 4 == to)
                def _():
                    t_out[n, d - 1] = x_keep[n, h].astype(BF)
                    zo(n, d).start()

    def st_m(n):
        b, q = n // 2, n % 2

        @pl.when(mine(b))
        def _():
            tot = x_keep[n, zl // 2]
            arrived(t_in.at[n], zo_r.at[n])
            for d in range(3):
                tot = tot + t_in[n, d].astype(F32)
            out[b // 2, :, half(q)] = tot.astype(BF)

    def gw_out(t):
        rows = pl.ds(t * TILE if isinstance(t, int) else pl.multiple_of(t * TILE, TILE), TILE)
        return pltpu.make_async_copy(gwb.at[rows], gw_hbm.at[rows], gwsem.at[t])

    def gw_tile(t):
        o = pl.multiple_of(t * TILE, TILE)
        lhs = xs[:NB, :, :, :, :, pl.ds(o, TILE)].reshape(1024, TILE)
        for p in range(2):
            rhs = jnp.concatenate([gp[2 * b + p].reshape(256, HALF) for b in range(NB)], axis=0)
            acc = lax.dot_general(lhs, rhs, (((0,), (0,)), ((), ())), preferred_element_type=F32)
            gwb[pl.ds(o, TILE), p * HALF : (p + 1) * HALF] = acc.astype(BF)
        gw_out(t).start()

    stages = dict(z=st_z, a=st_a, c=st_c, d=st_d, e=st_e, f=st_f, g=st_g, h=st_h, i=st_i, j=st_j, k=st_k, l=st_l, m=st_m)

    xs[NB] = jnp.zeros((4, 2, 2, BLK, 1536), BF)
    gp[NS] = jnp.zeros((4, 2, 2, BLK, HALF), BF)
    gp[NS + 1] = jnp.zeros((4, 2, 2, BLK, HALF), BF)

    @pl.loop(0, NSLOTS)
    def _(slot):
        for name, first in ORDER:
            n = slot - first
            go_now = (n >= 0) & (n < NS)
            if name in DRY:
                go_now = go_now | (slot == DRY[name])
                n = jnp.where(slot == DRY[name], NS, n)
            if name in "zac":
                go_now = go_now & (n % 2 == 0)
                n = n // 2

            @pl.when(go_now)
            def _():
                stages[name](n)

        @pl.when((slot >= GW_FIRST) & (slot < GW_FIRST + 6 // GW_EACH))
        def _():
            @pl.loop(0, GW_EACH)
            def _(t):
                gw_tile((slot - GW_FIRST) * GW_EACH + t)

    for b in range(NB):
        @pl.when(mine(b))
        def _():
            sent(xs.at[b, pl.ds(0, 3), 0, 0], zi_s.at[b])

    for n in range(NS):
        @pl.when(mine(n // 2))
        def _():
            sent(t_out.at[n, 0], zo_s.at[n])

        @pl.when(jnp.logical_not(mine(n // 2)))
        def _():
            sent(t_out.at[n, pl.ds(0, 2)], zo_s.at[n])

    sent(xs.at[pl.ds(0, NB), pl.ds(0, 3), 0], xi_s)
    sent(xs.at[pl.ds(0, NB), :, 0], si_s)
    sent(pb.at[pl.ds(0, NS), pl.ds(0, 12)], abc_s)
    sent(zs, zr_s)
    sent(gp.at[pl.ds(0, NS), 0, 0], zg_s)
    sent(gp.at[pl.ds(0, NS), pl.ds(0, 3)], g_s)
    sent(sib_out, so_s)
    sent(x_out, xo_s)

    for t in range(6):
        gw_out(t).wait()


def place(gi, gw, gi_out, gw_out, gi_buf, gw_buf, in_sem, out_sem):
    size = 1536 // PIECES
    ways = []
    for p in range(PIECES):
        rows = pl.ds(p * size, size)
        ways.append((gw.at[rows], gw_buf.at[rows], gw_out.at[rows]))
    ways.append((gi, gi_buf, gi_out))
    into = [pltpu.make_async_copy(src, buf, in_sem.at[p]) for p, (src, buf, _) in enumerate(ways)]
    onto = [pltpu.make_async_copy(buf, dst, out_sem.at[p]) for p, (_, buf, dst) in enumerate(ways)]
    for copy in into:
        copy.start()
    for first, second in zip(into, onto):
        first.wait()
        second.start()
    for copy in onto:
        copy.wait()


def per_device(inputs, weight, grad_out):
    any_ = pl.BlockSpec(memory_space=pl.ANY)
    vmem = pl.BlockSpec(memory_space=pltpu.VMEM)
    V = pltpu.VMEM
    D = pltpu.SemaphoreType.DMA
    sems = [
        D((NB,)), D((NB, 2)),
        D, D((NB,)),
        D, D((NB,)),
        D, D((NS, 2)), D((NS,)),
        D, D((NS,)),
        D, D((NS,)),
        D, D((NS, 2)), D((NB,)),
        D, D((NS,)),
        D, D((NS,)),
        D((NS,)), D((NS,)),
    ]
    grad_inputs, grad_weight = pl.pallas_call(
        kernel,
        out_shape=(
            jax.ShapeDtypeStruct((2, BLK, 1536), BF),
            jax.ShapeDtypeStruct((1536, 1536), BF),
        ),
        in_specs=[vmem, any_, any_],
        out_specs=(vmem, any_),
        scratch_shapes=[
            V((1536, 1536), BF),
            V((2, 2, 2, BLK, 1536), BF),
            V((NB + 1, 4, 2, 2, BLK, 1536), BF),
            V((NS + 1, 16, BLK, HALF), F32),
            V((NS + 1, 16, BLK, HALF), BF),
            V((NS, 2, 2, BLK, HALF), BF),
            V((NS, 2, 2, 2, BLK, HALF), BF),
            V((NS, 2, BLK, HALF), F32),
            V((NS, 2, BLK, HALF), BF),
            V((NS, 2, BLK, HALF), BF),
            V((NS + 2, 4, 2, 2, BLK, HALF), BF),
            V((NS + 1, 16, BLK, HALF), F32),
            V((NS, 8, BLK, HALF), BF),
            V((NS, 8, BLK, HALF), BF),
            V((NS, 3, 2, BLK, HALF), BF),
            V((NS, 3, 2, BLK, HALF), BF),
            V((NS, 2, BLK, HALF), F32),
            V((NS, 3, BLK, HALF), BF),
            V((NS, 3, BLK, HALF), BF),
            V((1536, 1536), BF),
            D((NB,)), D, D, D((6,)),
            *sems,
        ],
        compiler_params=pltpu.CompilerParams(
            collective_id=0, has_side_effects=True, vmem_limit_bytes=60 * 2**20
        ),
        cost_estimate=pl.CostEstimate(flops=3 * 2 * 1024 * 1536 * 1536, bytes_accessed=10**7, transcendentals=128 * 1536),
    )(inputs.reshape(2, BLK, 1536), weight, grad_out.reshape(2, 2, 2, BLK, 1536))
    grad_inputs, grad_weight = pl.pallas_call(
        place,
        out_shape=(jax.ShapeDtypeStruct((2, BLK, 1536), BF), jax.ShapeDtypeStruct((1536, 1536), BF)),
        in_specs=[any_, any_],
        out_specs=(any_, any_),
        scratch_shapes=[V((2, BLK, 1536), BF), V((1536, 1536), BF), D((PIECES + 1,)), D((PIECES + 1,))],
        compiler_params=pltpu.CompilerParams(vmem_limit_bytes=60 * 2**20),
    )(grad_inputs, grad_weight)
    return grad_inputs.reshape(32, 1536), grad_weight


def solution(mesh):
    return jax.shard_map(
        per_device,
        mesh=mesh,
        in_specs=(P("col", "row"), P("row", "col"), P("row", "col")),
        out_specs=(P("col", "row"), P("row", "col")),
        check_vma=False,
    )
```

time: 499 us -> 100 us (0.20)
  waiting for transfers between devices: 441 us -> 0 us
  Pallas kernels: 0 us -> 99.4 us
  matrix products: 28.3 us -> 0 us
  between operations: 13.8 us -> 0.64 us
  local copies, waits for them, and re-layouts: 8.5 us -> 0 us
    reduce_scatter x2 -> x0, waiting for transfers between devices: 283 us -> none  [the longest x1 151 us: per_device(): lax.psum_scatter(jnp.dot(block, weight, preferred_element_type=jnp.float3...]
    all_gather x2 -> x0, waiting for transfers between devices: 158 us -> none  [the longest x1 89.8 us: per_device(): all_grad = lax.all_gather(grad_pre, 'row', axis=0, tiled=True)]
    pallas_call x0 -> x2, Pallas kernels: none -> 99.4 us  [the longest x1 95.3 us: per_device(): pl.pallas_call(kernel, out_shape=(jax.ShapeDtypeStruct((2, BLK, 1536), BF...]
    dot_general x3 -> x0, matrix products: 28.3 us -> none  [the longest x1 9.78 us: per_device(): lax.dot_general(block, weight, (((1,), (1,)), ((), ())), preferred_elemen...]
    unnamed x5 -> x0, local copies, waits for them, and re-layouts: 8.5 us -> none
  transfers between devices with their start and end apart: 4 -> 0, of which waited for: 4 -> 0; matrix products, arithmetic and copies ran while one was open for 3% -> 0% of each run, Pallas kernels for 0% -> 0%
where the time goes in v2:
time: 100 us
  Pallas kernels  99.4 us (99%)
    pallas_call x1, Pallas kernels, per_device(): pl.pallas_call(kernel, out_shape=(jax.ShapeDtypeStruct((2, BLK, 1536), BF...  95.3 us
    pallas_call x1, Pallas kernels, per_device(): pl.pallas_call(place, out_shape=(jax.ShapeDtypeStruct((2, BLK, 1536), BF)...  4.16 us

profile of v2, /device:TPU:1, one launch (start us, length us, event | category | flops | bytes accessed | tf_op | source)
XLA Modules:
  0.0 100.0 jit_solution(11230857529833870737)
XLA Ops:
  0.6 95.3 %shard_map.50 = (bf16[2,16,1536]{2,1,0:T(8,128)(2,1)}, bf16[1536,1536]{1,0:T(8,128)(2,1)}) custom-call(bf16[2,16,1536]{2,1,0:T(8,128)(2,1)} %bitcast.4, bf16[1536,1536]{1,0:T(8,128)(2,1)} %w_hbm.1, bf16[2,2,2,16,1536]{4,3,2,1,0:T(8,128)(2,1)} %bitcast.3), custom_call_target="tpu_custom_call" | custom-call | flops 14495514624 | bytes 10000000 | tf_op jit(solution)/shard_map/pallas_call | solution.py:416
  95.9 4.2 %shard_map.51 = (bf16[2,16,1536]{2,1,0:T(8,128)(2,1)}, bf16[1536,1536]{1,0:T(8,128)(2,1)}) custom-call(bf16[2,16,1536]{2,1,0:T(8,128)(2,1)} %get-tuple-element.6.gi, bf16[1536,1536]{1,0:T(8,128)(2,1)} %get-tuple-element.7.gw), custom_call_target="tpu_custom_call" | custom-call | tf_op jit(solution)/shard_map/pallas_call | solution.py:453

commit v3 on v2

--- a/solution.py
+++ b/solution.py
@@ -18,8 +18,7 @@
 HALF = 768
 NS = 2 * NB
 
-ORDER = (('h', 13), ('e', 8), ('l', 21), ('j', 17), ('g', 11), ('k', 18), ('m', 37), ('i', 14), ('f', 9), ('d', 6), ('a', 2), ('c', 5), ('z', 0))
-DRY = {'d': 5, 'j': 6}
+ORDER = (('h', 13), ('e', 8), ('l', 21), ('j', 17), ('g', 11), ('k', 18), ('m', 29), ('i', 14), ('f', 9), ('d', 6), ('a', 2), ('c', 5), ('z', 0))
 NSLOTS = max(first for _, first in ORDER) + NS
 GW_FIRST = dict(ORDER)["j"] + NS - 1
 GW_EACH = 2
@@ -177,28 +176,23 @@
     def st_d(n):
         b, q = n // 2, n % 2
 
-        @pl.when((q == 0) & (n < NS))
+        @pl.when(q == 0)
         def _():
             arrived(xs.at[b, :, 1 - k], si_r.at[b])
 
-        @pl.when(n == NS)
+        @pl.when(n == 0)
         def _():
             w_cp.wait()
 
-        @pl.loop(0, jnp.where(n < NS, HALF // TILE, 1))
-        def _(t):
-            cols = pl.ds(pl.multiple_of(t * TILE, TILE), TILE)
-            acc = jnp.dot(xs[b].reshape(256, 1536), w[:, half(q, t, TILE)], preferred_element_type=F32)
-            acc = acc.reshape(16, BLK, TILE)
-            p32[n, :, :, cols] = acc
-            pb[n, :, :, cols] = acc.astype(BF)
-
-        @pl.when(n < NS)
-        def _():
-            for i in range(2):
-                a_cp(n, i).start()
-            for i in range(2):
-                b_cp(n, i).start()
+        acc = jnp.dot(xs[b].reshape(256, 1536), w[:, half(q)], preferred_element_type=F32)
+        acc = acc.reshape(16, BLK, HALF)
+        p32[n] = acc
+        pb[n] = acc.astype(BF)
+
+        for i in range(2):
+            a_cp(n, i).start()
+        for i in range(2):
+            b_cp(n, i).start()
 
     def st_e(n):
         for i in range(2):
@@ -250,11 +244,11 @@
     def st_j(n):
         b, q = n // 2, n % 2
 
-        @pl.when((q == 0) & (n < NS))
+        @pl.when(q == 0)
         def _():
             arrived(gp.at[pl.ds(2 * b, 2), pl.ds(0, 2)], gbc_r.at[b])
 
-        @pl.loop(0, jnp.where(n < NS, HALF // TILE, 1))
+        @pl.loop(0, HALF // TILE)
         def _(t):
             rows = half(q, t, TILE)
             acc = 0.0
@@ -267,11 +261,9 @@
                 )
             g32[n, :, :, pl.ds(pl.multiple_of(t * TILE, TILE), TILE)] = acc.reshape(16, BLK, TILE)
 
-        @pl.when(n < NS)
-        def _():
-            for g in range(4):
-                sib_out[n, pl.ds(2 * g, 2)] = g32[n, gk(g, 1 - k)].astype(BF)
-            so(n).start()
+        for g in range(4):
+            sib_out[n, pl.ds(2 * g, 2)] = g32[n, gk(g, 1 - k)].astype(BF)
+        so(n).start()
 
     def st_k(n):
         arrived(sib_in.at[n], so_r.at[n])
@@ -316,7 +308,7 @@
 
     def gw_tile(t):
         o = pl.multiple_of(t * TILE, TILE)
-        lhs = xs[:NB, :, :, :, :, pl.ds(o, TILE)].reshape(1024, TILE)
+        lhs = xs[:, :, :, :, :, pl.ds(o, TILE)].reshape(1024, TILE)
         for p in range(2):
             rhs = jnp.concatenate([gp[2 * b + p].reshape(256, HALF) for b in range(NB)], axis=0)
             acc = lax.dot_general(lhs, rhs, (((0,), (0,)), ((), ())), preferred_element_type=F32)
@@ -325,18 +317,11 @@
 
     stages = dict(z=st_z, a=st_a, c=st_c, d=st_d, e=st_e, f=st_f, g=st_g, h=st_h, i=st_i, j=st_j, k=st_k, l=st_l, m=st_m)
 
-    xs[NB] = jnp.zeros((4, 2, 2, BLK, 1536), BF)
-    gp[NS] = jnp.zeros((4, 2, 2, BLK, HALF), BF)
-    gp[NS + 1] = jnp.zeros((4, 2, 2, BLK, HALF), BF)
-
     @pl.loop(0, NSLOTS)
     def _(slot):
         for name, first in ORDER:
             n = slot - first
             go_now = (n >= 0) & (n < NS)
-            if name in DRY:
-                go_now = go_now | (slot == DRY[name])
-                n = jnp.where(slot == DRY[name], NS, n)
             if name in "zac":
                 go_now = go_now & (n % 2 == 0)
                 n = n // 2
@@ -424,16 +409,16 @@
         scratch_shapes=[
             V((1536, 1536), BF),
             V((2, 2, 2, BLK, 1536), BF),
-            V((NB + 1, 4, 2, 2, BLK, 1536), BF),
-            V((NS + 1, 16, BLK, HALF), F32),
-            V((NS + 1, 16, BLK, HALF), BF),
+            V((NB, 4, 2, 2, BLK, 1536), BF),
+            V((NS, 16, BLK, HALF), F32),
+            V((NS, 16, BLK, HALF), BF),
             V((NS, 2, 2, BLK, HALF), BF),
             V((NS, 2, 2, 2, BLK, HALF), BF),
             V((NS, 2, BLK, HALF), F32),
             V((NS, 2, BLK, HALF), BF),
             V((NS, 2, BLK, HALF), BF),
-            V((NS + 2, 4, 2, 2, BLK, HALF), BF),
-            V((NS + 1, 16, BLK, HALF), F32),
+            V((NS, 4, 2, 2, BLK, HALF), BF),
+            V((NS, 16, BLK, HALF), F32),
             V((NS, 8, BLK, HALF), BF),
             V((NS, 8, BLK, HALF), BF),
             V((NS, 3, 2, BLK, HALF), BF),

time: 100 us -> 98.5 us (0.985); the launches traced: 100 us -> 97.5 us
  Pallas kernels: 99.4 us -> 96.9 us
    pallas_call x1, Pallas kernels: 95.3 us -> 92.8 us  [per_device(): pl.pallas_call(kernel, out_shape=(jax.ShapeDtypeStruct((2, BLK, 1536), BF...]
where the time goes in v3:
time: 98.5 us; the launch traced here: 97.5 us
  Pallas kernels  96.9 us (98%)
    pallas_call x1, Pallas kernels, per_device(): pl.pallas_call(kernel, out_shape=(jax.ShapeDtypeStruct((2, BLK, 1536), BF...  92.8 us
    pallas_call x1, Pallas kernels, per_device(): pl.pallas_call(place, out_shape=(jax.ShapeDtypeStruct((2, BLK, 1536), BF)...  4.16 us

profile of v3, /device:TPU:1, one launch (start us, length us, event | category | flops | bytes accessed | tf_op | source)
XLA Modules:
  0.0 97.5 jit_solution(6824131729209533187)
XLA Ops:
  0.6 92.8 %shard_map.50 = (bf16[2,16,1536]{2,1,0:T(8,128)(2,1)}, bf16[1536,1536]{1,0:T(8,128)(2,1)}) custom-call(bf16[2,16,1536]{2,1,0:T(8,128)(2,1)} %bitcast.4, bf16[1536,1536]{1,0:T(8,128)(2,1)} %w_hbm.1, bf16[2,2,2,16,1536]{4,3,2,1,0:T(8,128)(2,1)} %bitcast.3), custom_call_target="tpu_custom_call" | custom-call | flops 14495514624 | bytes 10000000 | tf_op jit(solution)/shard_map/pallas_call | solution.py:401
  93.4 4.2 %shard_map.51 = (bf16[2,16,1536]{2,1,0:T(8,128)(2,1)}, bf16[1536,1536]{1,0:T(8,128)(2,1)}) custom-call(bf16[2,16,1536]{2,1,0:T(8,128)(2,1)} %get-tuple-element.6.gi, bf16[1536,1536]{1,0:T(8,128)(2,1)} %get-tuple-element.7.gw), custom_call_target="tpu_custom_call" | custom-call | tf_op jit(solution)/shard_map/pallas_call | solution.py:438

commit v4 on v3

--- a/solution.py
+++ b/solution.py
@@ -18,7 +18,7 @@
 HALF = 768
 NS = 2 * NB
 
-ORDER = (('h', 13), ('e', 8), ('l', 21), ('j', 17), ('g', 11), ('k', 18), ('m', 29), ('i', 14), ('f', 9), ('d', 6), ('a', 2), ('c', 5), ('z', 0))
+ORDER = (('h', 13), ('e', 8), ('l', 20), ('j', 16), ('g', 11), ('k', 17), ('m', 28), ('i', 14), ('f', 9), ('d', 6), ('a', 2), ('c', 5), ('z', 0))
 NSLOTS = max(first for _, first in ORDER) + NS
 GW_FIRST = dict(ORDER)["j"] + NS - 1
 GW_EACH = 2
@@ -132,11 +132,11 @@
 
     def gb(n, i):
         r = gp.at[n, y, 1 - i]
-        return rc(r, r, g_s, gbc_r.at[n // 2], (d_yp, d_ym)[i])
+        return rc(r, r, g_s, gbc_r.at[n], (d_yp, d_ym)[i])
 
     def gc(n, i):
         r = gp.at[n, (ym, yp)[i], i]
-        return rc(r, r, g_s, gbc_r.at[n // 2], (d_yp, d_ym)[i])
+        return rc(r, r, g_s, gbc_r.at[n], (d_yp, d_ym)[i])
 
     def so(n):
         return rc(sib_out.at[n], sib_in.at[n], so_s, so_r.at[n], d_sib)
@@ -153,7 +153,7 @@
     def st_z(b):
         @pl.when(mine(b))
         def _():
-            for d in (1, 2, 3):
+            for d in (2, 1, 3):
                 zi(b, d).start()
             own_copy(b).start()
 
@@ -243,27 +243,25 @@
 
     def st_j(n):
         b, q = n // 2, n % 2
-
-        @pl.when(q == 0)
-        def _():
-            arrived(gp.at[pl.ds(2 * b, 2), pl.ds(0, 2)], gbc_r.at[b])
-
-        @pl.loop(0, HALF // TILE)
-        def _(t):
-            rows = half(q, t, TILE)
-            acc = 0.0
-            for p in range(2):
-                acc += lax.dot_general(
-                    gp[2 * b + p].reshape(256, HALF),
-                    w[rows, p * HALF : (p + 1) * HALF],
-                    (((1,), (1,)), ((), ())),
-                    preferred_element_type=F32,
-                )
-            g32[n, :, :, pl.ds(pl.multiple_of(t * TILE, TILE), TILE)] = acc.reshape(16, BLK, TILE)
-
-        for g in range(4):
-            sib_out[n, pl.ds(2 * g, 2)] = g32[n, gk(g, 1 - k)].astype(BF)
-        so(n).start()
+        arrived(gp.at[n, pl.ds(0, 2)], gbc_r.at[n])
+
+        @pl.loop(0, 2)
+        def _(r):
+            m = 2 * b + r
+            acc = lax.dot_general(
+                gp[n].reshape(256, HALF), w[half(r), half(q)], (((1,), (1,)), ((), ())), preferred_element_type=F32
+            ).reshape(16, BLK, HALF)
+
+            @pl.when(q == 0)
+            def _():
+                g32[m] = acc
+
+            @pl.when(q == 1)
+            def _():
+                g32[m] += acc
+                for g in range(4):
+                    sib_out[m, pl.ds(2 * g, 2)] = g32[m, gk(g, 1 - k)].astype(BF)
+                so(m).start()
 
     def st_k(n):
         arrived(sib_in.at[n], so_r.at[n])
@@ -393,7 +391,7 @@
         D, D((NS, 2)), D((NS,)),
         D, D((NS,)),
         D, D((NS,)),
-        D, D((NS, 2)), D((NB,)),
+        D, D((NS, 2)), D((NS,)),
         D, D((NS,)),
         D, D((NS,)),
         D((NS,)), D((NS,)),

time: 98.5 us -> 97.7 us (level)
  no operation moved by 1% of the time
where the time goes in v4:
time: 97.7 us; the launch traced here: 97.6 us
  Pallas kernels  96.9 us (99%)
    pallas_call x1, Pallas kernels, per_device(): pl.pallas_call(kernel, out_shape=(jax.ShapeDtypeStruct((2, BLK, 1536), BF...  92.8 us
    pallas_call x1, Pallas kernels, per_device(): pl.pallas_call(place, out_shape=(jax.ShapeDtypeStruct((2, BLK, 1536), BF)...  4.16 us

profile of v4, /device:TPU:1, one launch (start us, length us, event | category | flops | bytes accessed | tf_op | source)
XLA Modules:
  0.0 97.6 jit_solution(14146696186456864146)
XLA Ops:
  0.6 92.8 %shard_map.50 = (bf16[2,16,1536]{2,1,0:T(8,128)(2,1)}, bf16[1536,1536]{1,0:T(8,128)(2,1)}) custom-call(bf16[2,16,1536]{2,1,0:T(8,128)(2,1)} %bitcast.4, bf16[1536,1536]{1,0:T(8,128)(2,1)} %w_hbm.1, bf16[2,2,2,16,1536]{4,3,2,1,0:T(8,128)(2,1)} %bitcast.3), custom_call_target="tpu_custom_call" | custom-call | flops 14495514624 | bytes 10000000 | tf_op jit(solution)/shard_map/pallas_call | solution.py:399
  93.4 4.2 %shard_map.51 = (bf16[2,16,1536]{2,1,0:T(8,128)(2,1)}, bf16[1536,1536]{1,0:T(8,128)(2,1)}) custom-call(bf16[2,16,1536]{2,1,0:T(8,128)(2,1)} %get-tuple-element.6.gi, bf16[1536,1536]{1,0:T(8,128)(2,1)} %get-tuple-element.7.gw), custom_call_target="tpu_custom_call" | custom-call | tf_op jit(solution)/shard_map/pallas_call | solution.py:436

commit v5 on v4

--- a/solution.py
+++ b/solution.py
@@ -20,7 +20,7 @@
 
 ORDER = (('h', 13), ('e', 8), ('l', 20), ('j', 16), ('g', 11), ('k', 17), ('m', 28), ('i', 14), ('f', 9), ('d', 6), ('a', 2), ('c', 5), ('z', 0))
 NSLOTS = max(first for _, first in ORDER) + NS
-GW_FIRST = dict(ORDER)["j"] + NS - 1
+GW_FIRST = dict(ORDER)["j"] + NS
 GW_EACH = 2
 
 

time: 97.7 us -> 97.7 us (level)
  no operation moved by 1% of the time
where the time goes in v5:
time: 97.7 us; the launch traced here: 97.6 us
  Pallas kernels  96.9 us (99%)
    pallas_call x1, Pallas kernels, per_device(): pl.pallas_call(kernel, out_shape=(jax.ShapeDtypeStruct((2, BLK, 1536), BF...  92.8 us
    pallas_call x1, Pallas kernels, per_device(): pl.pallas_call(place, out_shape=(jax.ShapeDtypeStruct((2, BLK, 1536), BF)...  4.16 us

profile of v5, /device:TPU:1, one launch (start us, length us, event | category | flops | bytes accessed | tf_op | source)
XLA Modules:
  0.0 97.6 jit_solution(10182321987709465265)
XLA Ops:
  0.6 92.8 %shard_map.50 = (bf16[2,16,1536]{2,1,0:T(8,128)(2,1)}, bf16[1536,1536]{1,0:T(8,128)(2,1)}) custom-call(bf16[2,16,1536]{2,1,0:T(8,128)(2,1)} %bitcast.4, bf16[1536,1536]{1,0:T(8,128)(2,1)} %w_hbm.1, bf16[2,2,2,16,1536]{4,3,2,1,0:T(8,128)(2,1)} %bitcast.3), custom_call_target="tpu_custom_call" | custom-call | flops 14495514624 | bytes 10000000 | tf_op jit(solution)/shard_map/pallas_call | solution.py:399
  93.4 4.2 %shard_map.51 = (bf16[2,16,1536]{2,1,0:T(8,128)(2,1)}, bf16[1536,1536]{1,0:T(8,128)(2,1)}) custom-call(bf16[2,16,1536]{2,1,0:T(8,128)(2,1)} %get-tuple-element.6.gi, bf16[1536,1536]{1,0:T(8,128)(2,1)} %get-tuple-element.7.gw), custom_call_target="tpu_custom_call" | custom-call | tf_op jit(solution)/shard_map/pallas_call | solution.py:436
